TPU v7x, 512 devices: a whole 4x4x16 slice. The times are simulated.
512 devices in a mesh: prompt: 16 (over z), seq: 32 (over y, x, core).
Axes of the slice: x: 4, y: 4, z: 16, core: 2. Of those that a mesh axis runs over, the one named last changes fastest.
Arguments:
- queries: bfloat16 [16, 32, 2, 32, 128], P('prompt', 'seq'), may hold values from -160 to 160
- prompt_key_cache: bfloat16 [16, 4, 8192, 128], P('prompt', None, 'seq'), may hold values from -5 to 5
- prompt_value_cache: bfloat16 [16, 4, 8192, 128], P('prompt', None, 'seq'), may hold values from -6 to 6
- kept: int32 [16, 4, 32], P('prompt', None, 'seq'), may hold values from 1 to 2, as said below
- sample_keys: bfloat16 [16, 32, 4, 256, 128], P('prompt', 'seq'), may hold values from -6 to 6
- sample_values: bfloat16 [16, 32, 4, 256, 128], P('prompt', 'seq'), may hold values from -6 to 6
- suffix_len: int32 [16, 32], P('prompt', 'seq'), may hold values from 1 to 256, as said below
- decode_keys: bfloat16 [16, 32, 2, 4, 128], P('prompt', 'seq'), may hold values from -6 to 6
- decode_values: bfloat16 [16, 32, 2, 4, 128], P('prompt', 'seq'), may hold values from -6 to 6
- out_weight: bfloat16 [4096, 8192], P('seq', 'prompt'), may hold values from -0.1875 to 0.1875
Outputs:
- attn_out: bfloat16 [1024, 8192], P('seq', 'prompt')
Inputs may be any that keep to these rules, and one draw needn't show every extreme that they name: `kept`: for every prompt and key-value head some seq index has all 2 slots live. `suffix_len`: in every prompt some sample has 256 generated tokens.
All inputs are finite; a program needn't handle non-finite values.
Results may differ from a plain program's by a relative error of at most 0.0048.
Values may be sent and summed in bfloat16 or wider, within the bound.
A program may use at most 128 MiB of HBM per device.

v0:
```python
import math
import jax
import jax.numpy as jnp
from jax import lax
from jax.sharding import PartitionSpec as P

BLOCK_TOKENS = 128
KEPT_SLOTS = 2
NEGATIVE = -1e30


def joined(x, axis, combine):
    everything = jax.tree.map(lambda part: lax.all_gather(part, axis), x)
    initial = jax.tree.map(lambda part: part[0], everything)

    def lap(k, so_far):
        return combine(so_far, jax.tree.map(lambda part: part[k], everything))

    return lax.fori_loop(1, lax.axis_size(axis), lap, initial)


def combine(earlier, later):
    highest = jnp.maximum(earlier[0], later[0])
    early_factor = jnp.exp(earlier[0] - highest)
    late_factor = jnp.exp(later[0] - highest)
    softmax_total = earlier[1] * early_factor + later[1] * late_factor
    summed = earlier[2] * early_factor[..., None] + later[2] * late_factor[..., None]
    return (highest, softmax_total, summed)


def on_device(
    queries,
    prompt_key_cache,
    prompt_value_cache,
    kept,
    sample_keys,
    sample_values,
    suffix_len,
    decode_keys,
    decode_values,
    out_weight,
):
    seq_count = lax.axis_size("seq")
    seq_index = lax.axis_index("seq")
    own_count = queries.shape[1]
    step_count = queries.shape[2]
    head_count = queries.shape[3]
    head_dim = queries.shape[4]
    kv_count = prompt_key_cache.shape[1]
    group_size = head_count // kv_count
    logit_scale = 1.0 / math.sqrt(head_dim)
    gathered = lax.all_gather(queries, "seq", axis=1, tiled=True)
    sample_count = gathered.shape[1]
    grouped_queries = gathered[0].reshape(sample_count, step_count, kv_count, group_size, head_dim)
    query_rows = jnp.transpose(grouped_queries, (2, 0, 1, 3, 4)).reshape(
        kv_count, sample_count * step_count * group_size, head_dim
    )
    key_cache_store = prompt_key_cache[0].reshape(kv_count, KEPT_SLOTS, BLOCK_TOKENS, head_dim)
    value_cache_store = prompt_value_cache[0].reshape(kv_count, KEPT_SLOTS, BLOCK_TOKENS, head_dim)
    kept_block_counts = kept[0, :, 0]
    active_mask = jnp.arange(KEPT_SLOTS, dtype=jnp.int32)[None, :] < kept_block_counts[:, None]

    def one_head(pieces):
        head_row_block, key_block_list, value_block_list, live_blocks = pieces
        logit_scores = (
            jnp.einsum(
                "eg,mxg->emx", head_row_block, key_block_list, preferred_element_type=jnp.float32
            )
            * logit_scale
        )
        block_max = jnp.where(live_blocks[None, :], jnp.max(logit_scores, axis=2), NEGATIVE)
        attention_weights = jnp.where(
            live_blocks[None, :, None], jnp.exp(logit_scores - block_max[:, :, None]), 0.0
        )
        block_sum = jnp.sum(attention_weights, axis=2)
        block_output = jnp.einsum(
            "yaf,afi->yai",
            attention_weights.astype(jnp.bfloat16),
            value_block_list,
            preferred_element_type=jnp.float32,
        )
        highest = jnp.max(block_max, axis=1)
        factor = jnp.exp(block_max - highest[:, None])
        return (
            highest,
            jnp.sum(factor * block_sum, axis=1),
            jnp.sum(factor[:, :, None] * block_output, axis=1),
        )

    prompt_maximum, prompt_sum, prompt_output = lax.map(
        one_head, (query_rows, key_cache_store, value_cache_store, active_mask)
    )
    own_queries = queries[0].reshape(own_count, step_count, kv_count, group_size, head_dim)
    suffix_scores = (
        jnp.einsum(
            "nthgd,nhid->nhtgi", own_queries, sample_keys[0], preferred_element_type=jnp.float32
        )
        * logit_scale
    )
    fresh_scores = (
        jnp.einsum(
            "nthgd,nuhd->nhtgu", own_queries, decode_keys[0], preferred_element_type=jnp.float32
        )
        * logit_scale
    )
    position = jnp.arange(sample_keys.shape[3], dtype=jnp.int32)
    sample_token_mask = (position[None, :] < suffix_len[0][:, None])[:, None, None, None, :]
    step_index = jnp.arange(step_count, dtype=jnp.int32)
    newest_token_mask = (step_index[None, :] <= step_index[:, None])[None, None, :, None, :]
    tail_max = jnp.maximum(
        jnp.max(jnp.where(sample_token_mask, suffix_scores, NEGATIVE), axis=4),
        jnp.max(jnp.where(newest_token_mask, fresh_scores, NEGATIVE), axis=4),
    )
    suffix_weights = jnp.where(sample_token_mask, jnp.exp(suffix_scores - tail_max[..., None]), 0.0)
    fresh_weights = jnp.where(newest_token_mask, jnp.exp(fresh_scores - tail_max[..., None]), 0.0)
    tail_sum = jnp.sum(suffix_weights, axis=4) + jnp.sum(fresh_weights, axis=4)
    tail_out = jnp.einsum(
        "nhtgi,nhid->nhtgd",
        suffix_weights.astype(jnp.bfloat16),
        sample_values[0],
        preferred_element_type=jnp.float32,
    )
    tail_out = tail_out + jnp.einsum(
        "nhtgu,nuhd->nhtgd",
        fresh_weights.astype(jnp.bfloat16),
        decode_values[0],
        preferred_element_type=jnp.float32,
    )
    tail_part = (
        jnp.transpose(tail_max, (1, 0, 2, 3)),
        jnp.transpose(tail_sum, (1, 0, 2, 3)),
        jnp.transpose(tail_out, (1, 0, 2, 3, 4)),
    )
    prefix = (
        prompt_maximum.reshape(kv_count, sample_count, step_count, group_size),
        prompt_sum.reshape(kv_count, sample_count, step_count, group_size),
        prompt_output.reshape(kv_count, sample_count, step_count, group_size, head_dim),
    )
    offset = seq_index * own_count
    own_part = tuple((lax.dynamic_slice_in_dim(member, offset, own_count, 1) for member in prefix))
    merged = combine(own_part, tail_part)
    prefix = tuple(
        (
            lax.dynamic_update_slice_in_dim(member, update, offset, 1)
            for member, update in zip(prefix, merged)
        )
    )
    part_max = jnp.transpose(prefix[0], (1, 2, 0, 3)).reshape(sample_count, step_count, head_count)
    part_total = jnp.transpose(prefix[1], (1, 2, 0, 3)).reshape(
        sample_count, step_count, head_count
    )
    part_out = jnp.transpose(prefix[2], (1, 2, 0, 3, 4)).reshape(
        sample_count, step_count, head_count, head_dim
    )
    local_heads = head_count // seq_count
    highest, softmax_total, summed = joined((part_max, part_total, part_out), "seq", combine)
    highest = lax.dynamic_slice_in_dim(highest, seq_index * local_heads, local_heads, 2)
    softmax_total = lax.dynamic_slice_in_dim(softmax_total, seq_index * local_heads, local_heads, 2)
    summed = lax.dynamic_slice_in_dim(summed, seq_index * local_heads, local_heads, 2)
    head_out = (
        (summed / softmax_total[..., None])
        .astype(jnp.bfloat16)
        .reshape(sample_count * step_count, local_heads * head_dim)
    )
    all_rows = lax.all_gather(head_out, "prompt", axis=0, tiled=True)
    result = lax.psum_scatter(
        jnp.dot(all_rows, out_weight, preferred_element_type=jnp.float32),
        "seq",
        scatter_dimension=0,
        tiled=True,
    )
    return result.astype(jnp.bfloat16)


def solution(mesh):
    placed = (
        P("prompt", "seq", None, None, None),
        P("prompt", None, "seq", None),
        P("prompt", None, "seq", None),
        P("prompt", None, "seq"),
        P("prompt", "seq", None, None, None),
        P("prompt", "seq", None, None, None),
        P("prompt", "seq"),
        P("prompt", "seq", None, None, None),
        P("prompt", "seq", None, None, None),
        P("seq", "prompt"),
    )
    return jax.shard_map(
        on_device, mesh=mesh, in_specs=placed, out_specs=P("seq", "prompt"), check_vma=False
    )
```

profile of v0, /device:TPU:2, one launch (start us, length us, event | category | flops | bytes accessed | tf_op | source)
XLA Modules:
  0.0 388.6 jit_solution(14444092180296759480)
XLA Ops:
  8.0 27.6 %all_gather.15 = bf16[1,32,2,32,128]{4,3,2,0,1:T(8,128)(2,1)S(1)} all-gather(bf16[1,1,2,32,128]{4,3,2,0,1:T(8,128)(2,1)} %bitcast.184), channel_id=1, replica_groups=mesh['prompt'=16,'seq'=32] {'seq'}, dimensions={1}, use_global_device_ids=true | all-gather | bytes 540672 | tf_op jit(solution)/shard_map/all_gather | solution.py:52
  35.7 11.2 %while.33 = (s32[]{:T(128)}, f32[4,512]{1,0:T(4,128)S(1)}, f32[4,512]{1,0:T(4,128)S(1)}, f32[4,512,128]{2,1,0:T(8,128)S(1)}, pred[4,2]{1,0:T(4,128)(4,1)S(1)}, /...) while((s32[]{:T(128)}, f32[4,512]{1,0:T(4,128)S(1)}, ...), condition=%wide.region_6.7_spmd, body=%wide.region_0.6_spmd.sunk | while | flops 68356096 | bytes 3202187 | solution.py:90
  53.4 22.9 %all_gather.16 = f32[32,32,2,32]{3,1,2,0:T(8,128)S(1)} all-gather(f32[1,32,2,32]{3,1,2,0:T(8,128)S(1)} %copy.49), channel_id=1, replica_groups=mesh['prompt'=16,'seq'=32] {'seq'}, dimensions={0}, use_global_device_ids=true | all-gather | bytes 270336 | tf_op jit(solution)/shard_map/all_gather | solution.py:13
  76.4 24.8 %all_gather.17 = f32[32,32,2,32]{3,1,2,0:T(8,128)S(1)} all-gather(f32[1,32,2,32]{3,1,2,0:T(8,128)S(1)} %copy.53), channel_id=1, replica_groups=mesh['prompt'=16,'seq'=32] {'seq'}, dimensions={0}, use_global_device_ids=true | all-gather | bytes 270336 | tf_op jit(solution)/shard_map/all_gather | solution.py:13
  101.2 82.0 %all-gather.2.cloned.1.call-done = f32[32,32,2,32,128]{4,3,2,1,0:T(8,128)} async-done(((f32[1,32,2,32,128]{4,3,2,1,0:T(8,128)}), f32[32,32,2,32,128]{4,3,2,1,0:T(8,128)}) %all-gather.2.cloned.1.call-update) | async-done | bytes 33554448 | tf_op jit(solution)/shard_map/all_gather | solution.py:13
  184.5 63.3 %while.34 = (s32[]{:T(128)}, f32[32,2,32]{2,1,0:T(2,128)S(1)}, f32[32,2,32]{2,1,0:T(2,128)S(1)}, f32[32,2,32,128]{3,2,1,0:T(8,128)S(1)}, f32[32,32,2,32]{3,1,2,0...) while((s32[]{:T(128)}, f32[32,2,32]{2,1,0:T(2,128)S(1)}, ...), condition=%wide.region_12.13_spmd, body=%wide.region_11.12_spmd.sunk | while | flops 798725 | bytes 3260559 | solution.py:19
  184.6 1.9 fusion.72
  186.7 1.9 fusion.72
  188.7 1.9 fusion.72
  190.8 1.9 fusion.72
  192.8 1.9 fusion.72
  194.9 1.9 fusion.72
  196.9 1.9 fusion.72
  198.9 1.9 fusion.72
  201.0 1.9 fusion.72
  203.0 1.9 fusion.72
  205.1 1.9 fusion.72
  207.1 1.9 fusion.72
  209.2 1.9 fusion.72
  211.2 1.9 fusion.72
  213.2 1.9 fusion.72
  215.3 1.9 fusion.72
  217.3 1.9 fusion.72
  219.4 1.9 fusion.72
  221.4 1.9 fusion.72
  223.4 1.9 fusion.72
  225.5 1.9 fusion.72
  227.5 1.9 fusion.72
  229.6 1.9 fusion.72
  248.3 31.6 %all_gather.19 = bf16[1024,128]{1,0:T(8,128)(2,1)S(1)} all-gather(bf16[64,128]{1,0:T(8,128)(2,1)S(1)} %bitcast.185), channel_id=1, replica_groups=mesh['prompt'=16,'seq'=32] {'prompt'}, dimensions={0}, use_global_device_ids=true | all-gather | bytes 278528 | tf_op jit(solution)/shard_map/all_gather | solution.py:165
  279.9 2.7 fusion.51
  282.6 97.6 %reduce-scatter.2.cloned.1.call-done = f32[32,512]{1,0:T(8,128)} async-done(((f32[1024,512]{1,0:T(8,128)}), f32[32,512]{1,0:T(8,128)}) %reduce-scatter.2.cloned.1.call-update) | async-done | bytes 65552 | tf_op jit(solution)/shard_map/reduce_scatter | solution.py:166
  (150 shorter events, 40.3 us)
Async XLA Ops:
  6.5 41.6 %copy-start = (bf16[1,1,4,256,128]{4,3,2,1,0:T(8,128)(2,1)S(1)}, bf16[1,1,4,256,128]{4,3,2,1,0:T(8,128)(2,1)}, u32[]{:S(2)}) copy-start(bf16[1,1,4,256,128]{4,3,2,1,0:T(8,128)(2,1)} %param.18) | copy-start | bytes 786436
  6.5 176.7 %all-gather.2.cloned.1.call-start = ((), (), s32[]{:S(2)}) async-start(), calls=%async_computation.1 | async-start | bytes 34603008 | tf_op jit(solution)/shard_map/all_gather | solution.py:13
  53.0 327.3 %reduce-scatter.2.cloned.1.call-start = ((), (), s32[]{:S(2)}) async-start(), calls=%async_computation.2 | async-start | bytes 2162688 | tf_op jit(solution)/shard_map/reduce_scatter | solution.py:166
Sparse Core Ops, SparseCore 0:
  53.1 130.0 all-gather.1
  282.7 97.4 reduce-scatter.1
where the time goes:
time: 391 us; the launch traced here: 389 us
  waiting for transfers between devices  180 us (46%)
  blocking collectives  107 us (27%)
  other arithmetic  65.6 us (17%)
  matrix products  15.6 us (4%)
  between operations  14.2 us (4%)
  local copies, waits for them, and re-layouts  5.13 us (1%)
    reduce_scatter x1, waiting for transfers between devices, on_device(): lax.psum_scatter(jnp.dot(all_rows, out_weight, preferred_element_type=jnp...  97.6 us
    all_gather x1, waiting for transfers between devices, joined(): everything = jax.tree.map(lambda part: lax.all_gather(part, axis), x)  82 us
    add x31, other arithmetic, combine(): earlier[2] * early_factor[..., None] + later[2] * late_factor[..., None]  58.6 us
    all_gather x2, blocking collectives, joined(): everything = jax.tree.map(lambda part: lax.all_gather(part, axis), x)  47.8 us
    all_gather x1, blocking collectives, on_device(): all_rows = lax.all_gather(head_out, 'prompt', axis=0, tiled=True)  31.6 us
    all_gather x1, blocking collectives, on_device(): gathered = lax.all_gather(queries, 'seq', axis=1, tiled=True)  27.6 us
  transfers between devices with their start and end apart: 2, of which 2 were waited for; matrix products, arithmetic and copies ran while one was open for 0% of the time, Pallas kernels for 0%

commit v1 on v0

--- a/solution.py
+++ b/solution.py
@@ -7,6 +7,22 @@
 BLOCK_TOKENS = 128
 KEPT_SLOTS = 2
 NEGATIVE = -1e30
+
+
+def gather_around(x, axis, dim):
+    ways, here, step = (lax.axis_size(axis), lax.axis_index(axis), x.shape[dim])
+    dims = [n * ways if d == dim else n for d, n in enumerate(x.shape)]
+    full = lax.dynamic_update_slice_in_dim(jnp.zeros(dims, x.dtype), x, here * step, axis=dim)
+    going_up = going_down = x
+    for far in range(1, ways // 2 + 1):
+        going_up = lax.ppermute(going_up, axis, [(d, (d + 1) % ways) for d in range(ways)])
+        full = lax.dynamic_update_slice_in_dim(full, going_up, (here - far) % ways * step, axis=dim)
+        if 2 * far < ways:
+            going_down = lax.ppermute(going_down, axis, [(d, (d - 1) % ways) for d in range(ways)])
+            full = lax.dynamic_update_slice_in_dim(
+                full, going_down, (here + far) % ways * step, axis=dim
+            )
+    return full
 
 
 def joined(x, axis, combine):
@@ -162,7 +178,7 @@
         .astype(jnp.bfloat16)
         .reshape(sample_count * step_count, local_heads * head_dim)
     )
-    all_rows = lax.all_gather(head_out, "prompt", axis=0, tiled=True)
+    all_rows = gather_around(head_out, "prompt", 0)
     result = lax.psum_scatter(
         jnp.dot(all_rows, out_weight, preferred_element_type=jnp.float32),
         "seq",

time: 391 us -> 420 us (1.074)
  starting transfers between devices: 0.04 us -> 52.2 us
  blocking collectives: 107 us -> 75.7 us
  waiting for transfers between devices: 180 us -> 187 us
    ppermute x0 -> x15, starting transfers between devices: none -> 52.1 us  [the longest x7 35.2 us: gather_around(): lax.ppermute(going_down, axis, [(d, (d - 1) % ways) for d in range(ways)])]
    all_gather x1 -> x0, blocking collectives: 31.6 us -> none  [on_device(): all_rows = lax.all_gather(head_out, 'prompt', axis=0, tiled=True)]
    ppermute x0 -> x15, waiting for transfers between devices: none -> 4.91 us  [the longest x8 4.89 us: gather_around(): lax.ppermute(going_up, axis, [(d, (d + 1) % ways) for d in range(ways)])]
  transfers between devices with their start and end apart: 2 -> 17, of which waited for: 2 -> 3; matrix products, arithmetic and copies ran while one was open for 0% -> 0% of each run, Pallas kernels for 0% -> 0%
where the time goes in v1:
time: 420 us; the launch traced here: 417 us
  waiting for transfers between devices  187 us (45%)
  blocking collectives  75.7 us (18%)
  other arithmetic  65.6 us (16%)
  starting transfers between devices  52.2 us (12%)
  matrix products  15.6 us (4%)
  between operations  14.8 us (4%)
  local copies, waits for them, and re-layouts  5.43 us (1%)
    reduce_scatter x1, waiting for transfers between devices, on_device(): lax.psum_scatter(jnp.dot(all_rows, out_weight, preferred_element_type=jnp...  100 us
    all_gather x1, waiting for transfers between devices, joined(): everything = jax.tree.map(lambda part: lax.all_gather(part, axis), x)  81.4 us
    add x31, other arithmetic, combine(): earlier[2] * early_factor[..., None] + later[2] * late_factor[..., None]  58.6 us
    all_gather x2, blocking collectives, joined(): everything = jax.tree.map(lambda part: lax.all_gather(part, axis), x)  47.9 us
    ppermute x7, starting transfers between devices, gather_around(): lax.ppermute(going_down, axis, [(d, (d - 1) % ways) for d in range(ways)])  35.2 us
    all_gather x1, blocking collectives, on_device(): gathered = lax.all_gather(queries, 'seq', axis=1, tiled=True)  27.8 us
    ppermute x8, starting transfers between devices, gather_around(): lax.ppermute(going_up, axis, [(d, (d + 1) % ways) for d in range(ways)])  16.9 us
  transfers between devices with their start and end apart: 17, of which 3 were waited for; matrix products, arithmetic and copies ran while one was open for 0% of the time, Pallas kernels for 0%

profile of v1, /device:TPU:2, one launch (start us, length us, event | category | flops | bytes accessed | tf_op | source)
XLA Modules:
  0.0 417.2 jit_solution(3367016709007059453)
XLA Ops:
  6.6 27.8 %all_gather.12 = bf16[1,32,2,32,128]{4,3,2,0,1:T(8,128)(2,1)S(1)} all-gather(bf16[1,1,2,32,128]{4,3,2,0,1:T(8,128)(2,1)} %bitcast.182), channel_id=1, replica_groups=mesh['prompt'=16,'seq'=32] {'seq'}, dimensions={1}, use_global_device_ids=true | all-gather | bytes 540672 | tf_op jit(solution)/shard_map/all_gather | solution.py:68
  35.2 11.2 %while.33 = (s32[]{:T(128)}, f32[4,512]{1,0:T(4,128)S(1)}, f32[4,512]{1,0:T(4,128)S(1)}, f32[4,512,128]{2,1,0:T(8,128)S(1)}, pred[4,2]{1,0:T(4,128)(4,1)S(1)}, /...) while((s32[]{:T(128)}, f32[4,512]{1,0:T(4,128)S(1)}, ...), condition=%wide.region_6.7_spmd, body=%wide.region_0.6_spmd.sunk | while | flops 68356096 | bytes 3202687 | solution.py:106
  53.5 23.0 %all_gather.13 = f32[32,32,2,32]{3,1,2,0:T(8,128)S(1)} all-gather(f32[1,32,2,32]{3,1,2,0:T(8,128)S(1)} %copy.49), channel_id=1, replica_groups=mesh['prompt'=16,'seq'=32] {'seq'}, dimensions={0}, use_global_device_ids=true | all-gather | bytes 270336 | tf_op jit(solution)/shard_map/all_gather | solution.py:29
  76.7 24.9 %all_gather.14 = f32[32,32,2,32]{3,1,2,0:T(8,128)S(1)} all-gather(f32[1,32,2,32]{3,1,2,0:T(8,128)S(1)} %copy.53), channel_id=1, replica_groups=mesh['prompt'=16,'seq'=32] {'seq'}, dimensions={0}, use_global_device_ids=true | all-gather | bytes 270336 | tf_op jit(solution)/shard_map/all_gather | solution.py:29
  101.7 81.4 %all-gather.2.cloned.1.call-done = f32[32,32,2,32,128]{4,3,2,1,0:T(8,128)} async-done(((f32[1,32,2,32,128]{4,3,2,1,0:T(8,128)}), f32[32,32,2,32,128]{4,3,2,1,0:T(8,128)}) %all-gather.2.cloned.1.call-update) | async-done | bytes 33554448 | tf_op jit(solution)/shard_map/all_gather | solution.py:29
  184.4 63.4 %while.34 = (s32[]{:T(128)}, f32[32,2,32]{2,1,0:T(2,128)S(1)}, f32[32,2,32]{2,1,0:T(2,128)S(1)}, f32[32,2,32,128]{3,2,1,0:T(8,128)S(1)}, f32[32,32,2,32]{3,1,2,0...) while((s32[]{:T(128)}, f32[32,2,32]{2,1,0:T(2,128)S(1)}, ...), condition=%wide.region_12.13_spmd, body=%wide.region_11.12_spmd.sunk | while | flops 798725 | bytes 3260567 | solution.py:35
  184.6 1.9 fusion.72
  186.6 1.9 fusion.72
  188.7 1.9 fusion.72
  190.7 1.9 fusion.72
  192.8 1.9 fusion.72
  194.8 1.9 fusion.72
  196.8 1.9 fusion.72
  198.9 1.9 fusion.72
  248.3 3.5 collective-permute-start
  251.8 4.4 %collective-permute-start.1 = (bf16[64,128]{1,0:T(8,128)(2,1)S(1)}, bf16[64,128]{1,0:T(8,128)(2,1)S(1)}, u32[]{:S(2)}, u32[]{:S(2)}) collective-permute-start(bf16[64,128]{1,0:T(8,128)(2,1)S(1)} %bitcast.184), channel_id=1, source_target_pairs={{0,480},{32,0},{64,32},{96,64},{128,96},{160,128},{192,160},{224,1... | collective-permute-start | bytes 49160 | tf_op jit(solution)/shard_map/ppermute | solution.py:21
  256.2 1.9 collective-permute-start.2
  258.2 5.1 %collective-permute-start.3 = (bf16[64,128]{1,0:T(8,128)(2,1)S(1)}, bf16[64,128]{1,0:T(8,128)(2,1)S(1)}, u32[]{:S(2)}, u32[]{:S(2)}) collective-permute-start(bf16[64,128]{1,0:T(8,128)(2,1)S(1)} %collective-permute-done.1), channel_id=1, source_target_pairs={{0,480},{32,0},{64,32},{96,64},{128,96},{160,128},{192,160},{224,1... | collective-permute-start | bytes 49160 | tf_op jit(solution)/shard_map/ppermute | solution.py:21
  263.4 1.9 collective-permute-start.4
  265.3 5.1 %collective-permute-start.5 = (bf16[64,128]{1,0:T(8,128)(2,1)S(1)}, bf16[64,128]{1,0:T(8,128)(2,1)S(1)}, u32[]{:S(2)}, u32[]{:S(2)}) collective-permute-start(bf16[64,128]{1,0:T(8,128)(2,1)S(1)} %collective-permute-done.3), channel_id=1, source_target_pairs={{0,480},{32,0},{64,32},{96,64},{128,96},{160,128},{192,160},{224,1... | collective-permute-start | bytes 49160 | tf_op jit(solution)/shard_map/ppermute | solution.py:21
  270.5 1.9 collective-permute-start.6
  272.4 5.1 %collective-permute-start.7 = (bf16[64,128]{1,0:T(8,128)(2,1)S(1)}, bf16[64,128]{1,0:T(8,128)(2,1)S(1)}, u32[]{:S(2)}, u32[]{:S(2)}) collective-permute-start(bf16[64,128]{1,0:T(8,128)(2,1)S(1)} %collective-permute-done.5), channel_id=1, source_target_pairs={{0,480},{32,0},{64,32},{96,64},{128,96},{160,128},{192,160},{224,1... | collective-permute-start | bytes 49160 | tf_op jit(solution)/shard_map/ppermute | solution.py:21
  277.6 1.9 collective-permute-start.8
  279.6 5.1 %collective-permute-start.9 = (bf16[64,128]{1,0:T(8,128)(2,1)S(1)}, bf16[64,128]{1,0:T(8,128)(2,1)S(1)}, u32[]{:S(2)}, u32[]{:S(2)}) collective-permute-start(bf16[64,128]{1,0:T(8,128)(2,1)S(1)} %collective-permute-done.7), channel_id=1, source_target_pairs={{0,480},{32,0},{64,32},{96,64},{128,96},{160,128},{192,160},{224,1... | collective-permute-start | bytes 49160 | tf_op jit(solution)/shard_map/ppermute | solution.py:21
  284.7 1.9 collective-permute-start.10
  286.7 5.1 %collective-permute-start.11 = (bf16[64,128]{1,0:T(8,128)(2,1)S(1)}, bf16[64,128]{1,0:T(8,128)(2,1)S(1)}, u32[]{:S(2)}, u32[]{:S(2)}) collective-permute-start(bf16[64,128]{1,0:T(8,128)(2,1)S(1)} %collective-permute-done.9), channel_id=1, source_target_pairs={{0,480},{32,0},{64,32},{96,64},{128,96},{160,128},{192,160},{224,1... | collective-permute-start | bytes 49160 | tf_op jit(solution)/shard_map/ppermute | solution.py:21
  291.9 1.9 collective-permute-start.12
  293.8 5.1 %collective-permute-start.13 = (bf16[64,128]{1,0:T(8,128)(2,1)S(1)}, bf16[64,128]{1,0:T(8,128)(2,1)S(1)}, u32[]{:S(2)}, u32[]{:S(2)}) collective-permute-start(bf16[64,128]{1,0:T(8,128)(2,1)S(1)} %collective-permute-done.11), channel_id=1, source_target_pairs={{0,480},{32,0},{64,32},{96,64},{128,96},{160,128},{192,160},{224,1... | collective-permute-start | bytes 49160 | tf_op jit(solution)/shard_map/ppermute | solution.py:21
  299.0 1.9 collective-permute-start.14
  301.0 4.9 %collective-permute-done.14 = bf16[64,128]{1,0:T(8,128)(2,1)S(1)} collective-permute-done((bf16[64,128]{1,0:T(8,128)(2,1)S(1)}, bf16[64,128]{1,0:T(8,128)(2,1)S(1)}, u32[]{:S(2)}, u32[]{:S(2)}) %collective-permute-start.14) | collective-permute-done | bytes 16416 | tf_op jit(solution)/shard_map/ppermute | solution.py:18
  305.9 2.7 fusion.51
  308.5 100.4 %reduce-scatter.2.cloned.1.call-done = f32[32,512]{1,0:T(8,128)} async-done(((f32[1024,512]{1,0:T(8,128)}), f32[32,512]{1,0:T(8,128)}) %reduce-scatter.2.cloned.1.call-update) | async-done | bytes 65552 | tf_op jit(solution)/shard_map/reduce_scatter | solution.py:182
  (196 shorter events, 69.0 us)
Async XLA Ops:
  6.5 40.8 %copy-start = (bf16[1,1,4,256,128]{4,3,2,1,0:T(8,128)(2,1)S(1)}, bf16[1,1,4,256,128]{4,3,2,1,0:T(8,128)(2,1)}, u32[]{:S(2)}) copy-start(bf16[1,1,4,256,128]{4,3,2,1,0:T(8,128)(2,1)} %param.18) | copy-start | bytes 786436
  6.5 176.6 %all-gather.2.cloned.1.call-start = ((), (), s32[]{:S(2)}) async-start(), calls=%async_computation.1 | async-start | bytes 34603008 | tf_op jit(solution)/shard_map/all_gather | solution.py:29
  53.1 355.9 %reduce-scatter.2.cloned.1.call-start = ((), (), s32[]{:S(2)}) async-start(), calls=%async_computation.2 | async-start | bytes 2162688 | tf_op jit(solution)/shard_map/reduce_scatter | solution.py:182
  248.3 8.0 %collective-permute-start = (bf16[64,128]{1,0:T(8,128)(2,1)S(1)}, bf16[64,128]{1,0:T(8,128)(2,1)S(1)}, u32[]{:S(2)}, u32[]{:S(2)}) collective-permute-start(bf16[64,128]{1,0:T(8,128)(2,1)S(1)} %bitcast.183), channel_id=1, source_target_pairs={{0,32},{32,64},{64,96},{96,128},{128,160},{160,192},{192,224},{224... | collective-permute-start | bytes 49160 | tf_op jit(solution)/shard_map/ppermute | solution.py:18
  251.8 6.4 %collective-permute-start.1 = (bf16[64,128]{1,0:T(8,128)(2,1)S(1)}, bf16[64,128]{1,0:T(8,128)(2,1)S(1)}, u32[]{:S(2)}, u32[]{:S(2)}) collective-permute-start(bf16[64,128]{1,0:T(8,128)(2,1)S(1)} %bitcast.184), channel_id=1, source_target_pairs={{0,480},{32,0},{64,32},{96,64},{128,96},{160,128},{192,160},{224,1... | collective-permute-start | bytes 49160 | tf_op jit(solution)/shard_map/ppermute | solution.py:21
  256.2 7.1 %collective-permute-start.2 = (bf16[64,128]{1,0:T(8,128)(2,1)S(1)}, bf16[64,128]{1,0:T(8,128)(2,1)S(1)}, u32[]{:S(2)}, u32[]{:S(2)}) collective-permute-start(bf16[64,128]{1,0:T(8,128)(2,1)S(1)} %collective-permute-done), channel_id=1, source_target_pairs={{0,32},{32,64},{64,96},{96,128},{128,160},{160,192},{192,224},{224... | collective-permute-start | bytes 49160 | tf_op jit(solution)/shard_map/ppermute | solution.py:18
  258.2 7.1 %collective-permute-start.3 = (bf16[64,128]{1,0:T(8,128)(2,1)S(1)}, bf16[64,128]{1,0:T(8,128)(2,1)S(1)}, u32[]{:S(2)}, u32[]{:S(2)}) collective-permute-start(bf16[64,128]{1,0:T(8,128)(2,1)S(1)} %collective-permute-done.1), channel_id=1, source_target_pairs={{0,480},{32,0},{64,32},{96,64},{128,96},{160,128},{192,160},{224,1... | collective-permute-start | bytes 49160 | tf_op jit(solution)/shard_map/ppermute | solution.py:21
  263.4 7.1 %collective-permute-start.4 = (bf16[64,128]{1,0:T(8,128)(2,1)S(1)}, bf16[64,128]{1,0:T(8,128)(2,1)S(1)}, u32[]{:S(2)}, u32[]{:S(2)}) collective-permute-start(bf16[64,128]{1,0:T(8,128)(2,1)S(1)} %collective-permute-done.2), channel_id=1, source_target_pairs={{0,32},{32,64},{64,96},{96,128},{128,160},{160,192},{192,224},{224... | collective-permute-start | bytes 49160 | tf_op jit(solution)/shard_map/ppermute | solution.py:18
  265.3 7.1 %collective-permute-start.5 = (bf16[64,128]{1,0:T(8,128)(2,1)S(1)}, bf16[64,128]{1,0:T(8,128)(2,1)S(1)}, u32[]{:S(2)}, u32[]{:S(2)}) collective-permute-start(bf16[64,128]{1,0:T(8,128)(2,1)S(1)} %collective-permute-done.3), channel_id=1, source_target_pairs={{0,480},{32,0},{64,32},{96,64},{128,96},{160,128},{192,160},{224,1... | collective-permute-start | bytes 49160 | tf_op jit(solution)/shard_map/ppermute | solution.py:21
  270.5 7.1 %collective-permute-start.6 = (bf16[64,128]{1,0:T(8,128)(2,1)S(1)}, bf16[64,128]{1,0:T(8,128)(2,1)S(1)}, u32[]{:S(2)}, u32[]{:S(2)}) collective-permute-start(bf16[64,128]{1,0:T(8,128)(2,1)S(1)} %collective-permute-done.4), channel_id=1, source_target_pairs={{0,32},{32,64},{64,96},{96,128},{128,160},{160,192},{192,224},{224... | collective-permute-start | bytes 49160 | tf_op jit(solution)/shard_map/ppermute | solution.py:18
  272.4 7.1 %collective-permute-start.7 = (bf16[64,128]{1,0:T(8,128)(2,1)S(1)}, bf16[64,128]{1,0:T(8,128)(2,1)S(1)}, u32[]{:S(2)}, u32[]{:S(2)}) collective-permute-start(bf16[64,128]{1,0:T(8,128)(2,1)S(1)} %collective-permute-done.5), channel_id=1, source_target_pairs={{0,480},{32,0},{64,32},{96,64},{128,96},{160,128},{192,160},{224,1... | collective-permute-start | bytes 49160 | tf_op jit(solution)/shard_map/ppermute | solution.py:21
  277.6 7.1 %collective-permute-start.8 = (bf16[64,128]{1,0:T(8,128)(2,1)S(1)}, bf16[64,128]{1,0:T(8,128)(2,1)S(1)}, u32[]{:S(2)}, u32[]{:S(2)}) collective-permute-start(bf16[64,128]{1,0:T(8,128)(2,1)S(1)} %collective-permute-done.6), channel_id=1, source_target_pairs={{0,32},{32,64},{64,96},{96,128},{128,160},{160,192},{192,224},{224... | collective-permute-start | bytes 49160 | tf_op jit(solution)/shard_map/ppermute | solution.py:18
  279.6 7.1 %collective-permute-start.9 = (bf16[64,128]{1,0:T(8,128)(2,1)S(1)}, bf16[64,128]{1,0:T(8,128)(2,1)S(1)}, u32[]{:S(2)}, u32[]{:S(2)}) collective-permute-start(bf16[64,128]{1,0:T(8,128)(2,1)S(1)} %collective-permute-done.7), channel_id=1, source_target_pairs={{0,480},{32,0},{64,32},{96,64},{128,96},{160,128},{192,160},{224,1... | collective-permute-start | bytes 49160 | tf_op jit(solution)/shard_map/ppermute | solution.py:21
  284.7 7.1 %collective-permute-start.10 = (bf16[64,128]{1,0:T(8,128)(2,1)S(1)}, bf16[64,128]{1,0:T(8,128)(2,1)S(1)}, u32[]{:S(2)}, u32[]{:S(2)}) collective-permute-start(bf16[64,128]{1,0:T(8,128)(2,1)S(1)} %collective-permute-done.8), channel_id=1, source_target_pairs={{0,32},{32,64},{64,96},{96,128},{128,160},{160,192},{192,224},{224... | collective-permute-start | bytes 49160 | tf_op jit(solution)/shard_map/ppermute | solution.py:18
  286.7 7.1 %collective-permute-start.11 = (bf16[64,128]{1,0:T(8,128)(2,1)S(1)}, bf16[64,128]{1,0:T(8,128)(2,1)S(1)}, u32[]{:S(2)}, u32[]{:S(2)}) collective-permute-start(bf16[64,128]{1,0:T(8,128)(2,1)S(1)} %collective-permute-done.9), channel_id=1, source_target_pairs={{0,480},{32,0},{64,32},{96,64},{128,96},{160,128},{192,160},{224,1... | collective-permute-start | bytes 49160 | tf_op jit(solution)/shard_map/ppermute | solution.py:21
  291.9 7.1 %collective-permute-start.12 = (bf16[64,128]{1,0:T(8,128)(2,1)S(1)}, bf16[64,128]{1,0:T(8,128)(2,1)S(1)}, u32[]{:S(2)}, u32[]{:S(2)}) collective-permute-start(bf16[64,128]{1,0:T(8,128)(2,1)S(1)} %collective-permute-done.10), channel_id=1, source_target_pairs={{0,32},{32,64},{64,96},{96,128},{128,160},{160,192},{192,224},{224... | collective-permute-start | bytes 49160 | tf_op jit(solution)/shard_map/ppermute | solution.py:18
  293.8 7.1 %collective-permute-start.13 = (bf16[64,128]{1,0:T(8,128)(2,1)S(1)}, bf16[64,128]{1,0:T(8,128)(2,1)S(1)}, u32[]{:S(2)}, u32[]{:S(2)}) collective-permute-start(bf16[64,128]{1,0:T(8,128)(2,1)S(1)} %collective-permute-done.11), channel_id=1, source_target_pairs={{0,480},{32,0},{64,32},{96,64},{128,96},{160,128},{192,160},{224,1... | collective-permute-start | bytes 49160 | tf_op jit(solution)/shard_map/ppermute | solution.py:21
  299.0 6.8 %collective-permute-start.14 = (bf16[64,128]{1,0:T(8,128)(2,1)S(1)}, bf16[64,128]{1,0:T(8,128)(2,1)S(1)}, u32[]{:S(2)}, u32[]{:S(2)}) collective-permute-start(bf16[64,128]{1,0:T(8,128)(2,1)S(1)} %collective-permute-done.12), channel_id=1, source_target_pairs={{0,32},{32,64},{64,96},{96,128},{128,160},{160,192},{192,224},{224... | collective-permute-start | bytes 49160 | tf_op jit(solution)/shard_map/ppermute | solution.py:18
Sparse Core Ops, SparseCore 0:
  53.2 129.8 all-gather.1
  308.7 100.2 reduce-scatter.1
